TPU v7x, 32 devices: a whole 2x2x4 slice. The times are simulated.
32 devices in a mesh: groups: 2 (over y), cg: 16 (over z, x, core).
Axes of the slice: x: 2, y: 2, z: 4, core: 2. Of those that a mesh axis runs over, the one named last changes fastest.
Arguments:
- embeddings: bfloat16 [8192, 1024], P(('groups', 'cg')), parts along dimension 0, may hold values from -2000 to 2000
- destination: int32 [8192, 1], P(('groups', 'cg')), parts along dimension 0, may hold values from 0 to 15; in each aligned block of 256 rows (0 to 255, 256 to 511, ...) at most 32 rows name the same one
- valid_row: int32 [8192], P(('groups', 'cg')), parts along dimension 0, may hold values 0 or 1
Outputs:
- closest: float32 [8192], P(('groups', 'cg')), parts along dimension 0
There are 2 independent parts, one for each index of `groups`. A program takes and returns all parts, laid end to end along the dimension named above; each array names one. Nothing has to cross between parts.
Inputs may be any that keep to these rules, and one draw needn't show every extreme that they name: Among the documents of one device no destination appears more than 32 times, and some destination appears exactly 32 times on some device.
All inputs are finite; a program needn't handle non-finite values. No bound on the sum of `valid_row` on one device may be relied on, other than what follows from the above.
Results may differ from a plain program's by a relative error of at most 0.0005.
Values may be sent and summed in bfloat16 or wider, within the bound.
A program may use at most 64 MiB of HBM per device.

v0:
```python
import jax
import jax.numpy as jnp
from jax import lax
from jax.sharding import PartitionSpec as P

TEAM = 4


epsilon = 1e-06


def from_partner(array, axis, stride):
    return lax.ppermute(array, axis, [(i, i ^ 1 << stride) for i in range(lax.axis_size(axis))])


def normalize(embeddings):
    values = embeddings.astype(jnp.float32)
    inv_scale = lax.rsqrt(jnp.mean(values * values, axis=1, keepdims=True) + epsilon)
    return (values * inv_scale * values.shape[1] ** (-0.5)).astype(jnp.bfloat16)


def closest_in(own_rows, own_tag, own_key, other_rows, other_tag, other_key):
    similar = jnp.einsum("id,jd->ij", own_rows, other_rows, preferred_element_type=jnp.float32)
    matches = (
        (own_tag[:, None] == other_tag[None, :])
        & (own_tag[:, None] > 0)
        & (own_key[:, None] != other_key[None, :])
    )
    return jnp.max(jnp.where(matches, similar, -1.0), axis=1)


def on_device(embeddings, destination, valid_row):
    groups = lax.axis_size("cg")
    row_count, feat_width = embeddings.shape
    capacity = 2 * row_count // groups
    slot_count = groups * capacity
    member = lax.axis_index("cg") % TEAM
    unit_rows = normalize(embeddings)
    target = destination[:, 0]
    row_tag = jnp.where(valid_row == 1, 1, 0).astype(jnp.int32)
    places = jnp.arange(groups, dtype=jnp.int32)
    onehot = (target[:, None] == places[None, :]).astype(jnp.float32)
    row_order = jnp.arange(row_count, dtype=jnp.int32)
    earlier = (row_order[:, None] > row_order[None, :]).astype(jnp.float32)
    before = jnp.dot(earlier, onehot, precision=lax.Precision.HIGHEST)
    row_rank = jnp.sum(before * onehot, axis=1).astype(jnp.int32)
    row_slot = target * capacity + row_rank
    outgoing = jnp.zeros((slot_count, feat_width), jnp.bfloat16).at[row_slot].set(unit_rows)
    out_tags = jnp.zeros((slot_count,), jnp.int32).at[row_slot].set(row_tag)
    team_tags = jnp.repeat(out_tags.reshape(groups // TEAM, TEAM * capacity), TEAM, axis=0)
    positions = jnp.arange(slot_count, dtype=jnp.int32)
    own_key = member * slot_count + positions
    arrived, pool_tags = (
        lax.all_to_all(
            outgoing.reshape(groups, capacity, feat_width),
            "cg",
            split_axis=0,
            concat_axis=0,
            tiled=True,
        ),
        lax.all_to_all(team_tags, "cg", split_axis=0, concat_axis=0, tiled=True),
    )
    own_rows = arrived.reshape(slot_count, feat_width)

    def tags_of(owner_member):
        return lax.dynamic_slice_in_dim(pool_tags, owner_member * capacity, capacity, 1).reshape(
            slot_count
        )

    own_tag = tags_of(member)
    closest = closest_in(own_rows, own_tag, own_key, own_rows, own_tag, own_key)
    first_rows = from_partner(own_rows, "cg", 0)
    first_member = member ^ 1
    closest = jnp.maximum(
        closest,
        closest_in(
            own_rows,
            own_tag,
            own_key,
            first_rows,
            tags_of(first_member),
            first_member * slot_count + positions,
        ),
    )
    for held_rows, offset in ((own_rows, 2), (first_rows, 3)):
        far_rows = from_partner(held_rows, "cg", 1)
        owner_member = member ^ offset
        closest = jnp.maximum(
            closest,
            closest_in(
                own_rows,
                own_tag,
                own_key,
                far_rows,
                tags_of(owner_member),
                owner_member * slot_count + positions,
            ),
        )
    answers = lax.all_to_all(
        closest.reshape(groups, capacity), "cg", split_axis=0, concat_axis=0, tiled=True
    )
    return answers.reshape(slot_count)[row_slot]


def solution(mesh):
    return jax.shard_map(
        on_device,
        mesh=mesh,
        in_specs=(P(("groups", "cg"), None), P(("groups", "cg"), None), P(("groups", "cg"))),
        out_specs=P(("groups", "cg")),
        check_vma=False,
    )
```

profile of v0, /device:TPU:0, one launch (start us, length us, event | category | flops | bytes accessed | tf_op | source)
XLA Modules:
  0.0 109.3 jit_solution(11949734935041746187)
XLA Ops:
  0.0 0.0 copy-start.1
  0.0 0.0 copy-start
  0.0 0.7 copy-done.1
  0.7 0.2 fusion.4
  0.9 1.2 %fusion.5 = f32[256]{0:T(256)S(1)} fusion(bf16[256,1024]{1,0:T(8,128)(2,1)} %param.3), kind=kLoop, calls=%fused_computation.15 | loop fusion | flops 786176 | bytes 525312 | tf_op jit(solution)/shard_map/reduce_sum | solution.py:18
  2.1 0.0 copy-done
  2.1 2.0 %scatter_custom_fusion.1 = bf16[512,1024]{1,0:T(8,128)(2,1)S(1)} fusion(s32[256]{0:T(256)S(1)} %bitcast.25, bf16[256,1024]{1,0:T(8,128)(2,1)S(1)} %copy-done, f32[]{:T(128)} %constant.51.clone.1, f32[256]{0:T(256)S(1)} %add_rsqrt_fusion, bf16[]{:T(256)} %constant.14.clone.1), kind=kCustom, calls=%fused_computation.18 | custom fusion | flops 1048576 | bytes 1573894 | tf_op jit(solution)/shard_map/scatter | solution.py:48
  4.2 32.0 %all_to_all.20 = bf16[16,32,1024]{2,1,0:T(8,128)(2,1)S(1)} all-to-all(bf16[16,32,1024]{2,1,0:T(8,128)(2,1)S(1)} %bitcast.17), channel_id=1, replica_groups=mesh['groups'=2,'cg'=16] {'cg'}, dimensions={0} | all-to-all | bytes 2097152 | tf_op jit(solution)/shard_map/all_to_all | solution.py:54
  36.2 0.0 copy-start.2
  36.2 0.8 collective-permute-start
  36.9 0.0 copy-done.2
  37.0 1.4 %scatter_custom_fusion = s32[512]{0:T(512)S(1)} fusion(s32[256]{0:T(256)S(1)} %bitcast.26, s32[256]{0:T(256)S(1)} %compare_select_fusion.1, s32[]{:T(128)} %constant.16.clone.1), kind=kCustom, calls=%fused_computation.39 | custom fusion | bytes 2052 | tf_op jit(solution)/shard_map/scatter | solution.py:49
  38.4 0.6 broadcast_in_dim.18
  38.9 4.9 %all-to-all-start = ((s32[16,1,128]{2,1,0:T(1,128)}), s32[16,1,128]{2,1,0:T(1,128)S(1)}, u32[]{:S(2)}, u32[]{:S(2)}) async-start(s32[16,1,128]{2,1,0:T(1,128)} %bitcast.4), calls=%async_computation | async-start | bytes 16384 | tf_op jit(solution)/shard_map/all_to_all | solution.py:61
  43.9 1.9 %collective-permute-start.1 = (bf16[512,1024]{1,0:T(8,128)(2,1)S(1)}, bf16[512,1024]{1,0:T(8,128)(2,1)}, u32[]{:S(2)}, u32[]{:S(2)}) collective-permute-start(bf16[512,1024]{1,0:T(8,128)(2,1)S(1)} %bitcast.19), channel_id=1, source_target_pairs={{0,2},{1,3},{2,0},{3,1},{4,6},{5,7},{6,4},{7,5},{8,10},{9,11},{10,... | collective-permute-start | bytes 3145736 | tf_op jit(solution)/shard_map/ppermute | solution.py:13
  45.8 4.4 %all-to-all-done = s32[16,1,128]{2,1,0:T(1,128)S(1)} async-done(((s32[16,1,128]{2,1,0:T(1,128)}), s32[16,1,128]{2,1,0:T(1,128)S(1)}, u32[]{:S(2)}, u32[]{:S(2)}) %all-to-all-start) | async-done | bytes 8224 | tf_op jit(solution)/shard_map/all_to_all | solution.py:61
  50.3 0.2 dynamic-slice_reduce_fusion.2
  50.4 0.1 eq.87
  50.5 0.1 eq.83
  50.6 0.1 eq.93
  50.7 0.1 eq.90
  50.7 0.0 collective-permute-done
  50.7 0.5 collective-permute-start.2
  51.3 0.9 fusion
  52.1 0.9 fusion.1
  53.0 17.1 %collective-permute-done.1 = bf16[512,1024]{1,0:T(8,128)(2,1)} collective-permute-done((bf16[512,1024]{1,0:T(8,128)(2,1)S(1)}, bf16[512,1024]{1,0:T(8,128)(2,1)}, u32[]{:S(2)}, u32[]{:S(2)}) %collective-permute-start.1) | collective-permute-done | bytes 1048608 | tf_op jit(solution)/shard_map/ppermute | solution.py:13
  70.1 2.1 %fusion.2 = f32[512]{0:T(512)S(1)} fusion(bf16[512,1024]{1,0:T(8,128)(2,1)S(1)} %bitcast.22, bf16[512,1024]{1,0:T(8,128)(2,1)} %collective-permute-done.1, s32[512]{0:T(512)S(1)} %get-tuple-element.10, s32[512]{0:T(512)S(1)} %eq.83, s32[512]{0:T(512)S(1)} %iota_add_fusion.1, s32[512]{0:T(512)S(1)} %eq.90, pred[512]{0:T(512)(128)(4,1)S(1)} %broadcast_compare_fusion), kind=kOutput, calls=%fused_computation.11 | convolution fusion | flops 538443264 | bytes 2107904 | tf_op jit(solution)/shard_map/id,jd->ij/dot_general | solution.py:23
  72.2 19.8 %collective-permute-done.2 = bf16[512,1024]{1,0:T(8,128)(2,1)S(1)} collective-permute-done((bf16[512,1024]{1,0:T(8,128)(2,1)S(1)}, bf16[512,1024]{1,0:T(8,128)(2,1)S(1)}, u32[]{:S(2)}, u32[]{:S(2)}) %collective-permute-start.2) | collective-permute-done | bytes 1048608 | tf_op jit(solution)/shard_map/ppermute | solution.py:13
  92.0 0.9 fusion.3
  92.9 0.7 max.41
  93.6 5.5 %all-to-all-start.2 = ((f32[16,1,32]{2,1,0:T(1,128)}), f32[16,1,32]{2,1,0:T(1,128)S(1)}, u32[]{:S(2)}, u32[]{:S(2)}) async-start(f32[16,1,32]{2,1,0:T(1,128)} %max.41), calls=%async_computation.2 | async-start | bytes 16384 | tf_op jit(solution)/shard_map/all_to_all | solution.py:99
  99.1 6.4 %all-to-all-done.2 = f32[16,1,32]{2,1,0:T(1,128)S(1)} async-done(((f32[16,1,32]{2,1,0:T(1,128)}), f32[16,1,32]{2,1,0:T(1,128)S(1)}, u32[]{:S(2)}, u32[]{:S(2)}) %all-to-all-start.2) | async-done | bytes 2080 | tf_op jit(solution)/shard_map/all_to_all | solution.py:99
  105.5 0.5 broadcast.79
  106.0 0.7 reduce.19
  106.7 0.1 reshape.125
  106.8 2.5 %gather_fusion = f32[256]{0:T(256)} fusion(f32[512]{0:T(512)S(1)} %reshape.125, s32[1024]{0:T(1024)S(1)} %pad_clamp_fusion), kind=kCustom, calls=%fused_computation | custom fusion | bytes 3072 | tf_op jit(solution)/shard_map/gather | solution.py:102
  (10 shorter events, 0.1 us)
Async XLA Ops:
  0.0 0.7 copy-start.1
  0.0 2.1 %copy-start = (bf16[256,1024]{1,0:T(8,128)(2,1)S(1)}, bf16[256,1024]{1,0:T(8,128)(2,1)}, u32[]{:S(2)}) copy-start(bf16[256,1024]{1,0:T(8,128)(2,1)} %param.3) | copy-start | bytes 1572868
  36.2 0.8 copy-start.2
  36.2 14.6 %collective-permute-start = (bf16[512,1024]{1,0:T(8,128)(2,1)S(1)}, bf16[512,1024]{1,0:T(8,128)(2,1)S(1)}, u32[]{:S(2)}, u32[]{:S(2)}) collective-permute-start(bf16[512,1024]{1,0:T(8,128)(2,1)S(1)} %bitcast.18), channel_id=1, source_target_pairs={{0,1},{1,0},{2,3},{3,2},{4,5},{5,4},{6,7},{7,6},{8,9},{9,8},{10,11... | collective-permute-start | bytes 3145736 | tf_op jit(solution)/shard_map/ppermute | solution.py:13
  38.9 11.3 %all-to-all-start = ((s32[16,1,128]{2,1,0:T(1,128)}), s32[16,1,128]{2,1,0:T(1,128)S(1)}, u32[]{:S(2)}, u32[]{:S(2)}) async-start(s32[16,1,128]{2,1,0:T(1,128)} %bitcast.4), calls=%async_computation | async-start | bytes 16384 | tf_op jit(solution)/shard_map/all_to_all | solution.py:61
  43.9 26.2 %collective-permute-start.1 = (bf16[512,1024]{1,0:T(8,128)(2,1)S(1)}, bf16[512,1024]{1,0:T(8,128)(2,1)}, u32[]{:S(2)}, u32[]{:S(2)}) collective-permute-start(bf16[512,1024]{1,0:T(8,128)(2,1)S(1)} %bitcast.19), channel_id=1, source_target_pairs={{0,2},{1,3},{2,0},{3,1},{4,6},{5,7},{6,4},{7,5},{8,10},{9,11},{10,... | collective-permute-start | bytes 3145736 | tf_op jit(solution)/shard_map/ppermute | solution.py:13
  50.7 41.3 %collective-permute-start.2 = (bf16[512,1024]{1,0:T(8,128)(2,1)S(1)}, bf16[512,1024]{1,0:T(8,128)(2,1)S(1)}, u32[]{:S(2)}, u32[]{:S(2)}) collective-permute-start(bf16[512,1024]{1,0:T(8,128)(2,1)S(1)} %collective-permute-done), channel_id=1, source_target_pairs={{0,2},{1,3},{2,0},{3,1},{4,6},{5,7},{6,4},{7,5},{8,10},{9,11},{10,... | collective-permute-start | bytes 3145736 | tf_op jit(solution)/shard_map/ppermute | solution.py:13
  93.6 12.0 %all-to-all-start.2 = ((f32[16,1,32]{2,1,0:T(1,128)}), f32[16,1,32]{2,1,0:T(1,128)S(1)}, u32[]{:S(2)}, u32[]{:S(2)}) async-start(f32[16,1,32]{2,1,0:T(1,128)} %max.41), calls=%async_computation.2 | async-start | bytes 16384 | tf_op jit(solution)/shard_map/all_to_all | solution.py:99
where the time goes:
time: 110 us; the launch traced here: 109 us
  waiting for transfers between devices  47.7 us (43%)
  blocking collectives  32 us (29%)
  starting transfers between devices  13.6 us (12%)
  local copies, waits for them, and re-layouts  6.91 us (6%)
  matrix products  4.94 us (4%)
  other arithmetic  3.96 us (4%)
    ppermute x3, waiting for transfers between devices, from_partner(): lax.ppermute(array, axis, [(i, i ^ 1 << stride) for i in range(lax.axis_s...  36.9 us
    all_to_all x1, blocking collectives, on_device(): lax.all_to_all(outgoing.reshape(groups, capacity, feat_width), 'cg', spli...  32 us
    all_to_all x1, waiting for transfers between devices, on_device(): lax.all_to_all(closest.reshape(groups, capacity), 'cg', split_axis=0, con...  6.39 us
    all_to_all x1, starting transfers between devices, on_device(): lax.all_to_all(closest.reshape(groups, capacity), 'cg', split_axis=0, con...  5.54 us
    all_to_all x1, starting transfers between devices, on_device(): lax.all_to_all(team_tags, 'cg', split_axis=0, concat_axis=0, tiled=True)  4.9 us
    dot_general x4, matrix products, closest_in(): jnp.einsum('id,jd->ij', own_rows, other_rows, preferred_element_type=jnp....  4.74 us
    all_to_all x1, waiting for transfers between devices, on_device(): lax.all_to_all(team_tags, 'cg', split_axis=0, concat_axis=0, tiled=True)  4.45 us
    ppermute x3, starting transfers between devices, from_partner(): lax.ppermute(array, axis, [(i, i ^ 1 << stride) for i in range(lax.axis_s...  3.19 us
  transfers between devices with their start and end apart: 5, of which 4 were waited for; matrix products, arithmetic and copies ran while one was open for 6% of the time, Pallas kernels for 0%

commit v1 on v0

--- a/solution.py
+++ b/solution.py
@@ -1,6 +1,8 @@
 import jax
 import jax.numpy as jnp
 from jax import lax
+from jax.experimental import pallas as pl
+from jax.experimental.pallas import tpu as pltpu
 from jax.sharding import PartitionSpec as P
 
 TEAM = 4
@@ -102,9 +104,238 @@
     return answers.reshape(slot_count)[row_slot]
 
 
+MESH = pl.DeviceIdType.MESH
+PLANES = 4
+CHUNKS = 4
+TAG_ROWS = 16
+A, B, C = 4, 5, 6
+
+
+def pieces(row_count, feat_width):
+    step = row_count // CHUNKS
+    return [(row_count, TAG_ROWS, row_count)] + [(i * step, step, feat_width) for i in range(CHUNKS)]
+
+
+def kernel(emb_ref, tag_ref, out_ref, held, cols, outbox, inbox, send_sem, recv_sem, back_send, back_recv):
+    rows, width = emb_ref.shape
+    parts = pieces(rows, width)
+    group = lax.axis_index("groups")
+    me = lax.axis_index("cg")
+    z, p = me // TEAM, me % TEAM
+    core_p = p + 1 - 2 * (p % 2)
+    x_p = (p + 2) % TEAM
+    diag_p = (core_p + 2) % TEAM
+
+    def device(plane, place):
+        return (group, plane * TEAM + place)
+
+    barrier = pltpu.get_barrier_semaphore()
+    for k in range(1, TEAM):
+        pl.semaphore_signal(barrier, inc=1, device_id=device(z, (p + k) % TEAM), device_id_type=MESH)
+    for k in range(1, PLANES):
+        pl.semaphore_signal(barrier, inc=1, device_id=device((z + k) % PLANES, p), device_id_type=MESH)
+
+    for i in range(4):
+        block = pl.ds(i * (rows // 4), rows // 4)
+        values = emb_ref[block, :].astype(jnp.float32)
+        inv_scale = lax.rsqrt(jnp.mean(values * values, axis=1, keepdims=True) + epsilon)
+        held[p, block, :] = (values * inv_scale * width ** (-0.5)).astype(jnp.bfloat16)
+    held[p, pl.ds(rows, TAG_ROWS), pl.ds(0, rows)] = tag_ref[...]
+    pl.semaphore_wait(barrier, TEAM - 1 + PLANES - 1)
+
+    def piece(slot, k):
+        start, size, lanes = parts[k]
+        return held.at[slot, pl.ds(start, size), pl.ds(0, lanes)]
+
+    def copy(k, source, target, flow, to):
+        return pltpu.make_async_remote_copy(
+            src_ref=piece(source, k),
+            dst_ref=piece(target, k),
+            send_sem=send_sem.at[flow, k],
+            recv_sem=recv_sem.at[target, k],
+            device_id=to,
+            device_id_type=MESH,
+        )
+
+    up, down = (z + 1) % PLANES, (z + PLANES - 1) % PLANES
+    second = jnp.where(z == 1, B, A)
+    core_own = lambda k: copy(k, p, p, 0, device(z, core_p))
+    x_own = lambda k: copy(k, p, p, 1, device(z, x_p))
+    core_pass = lambda k: copy(k, x_p, x_p, 2, device(z, core_p))
+    up_own = lambda k: copy(k, p, A, 3, device(up, p))
+    up_first = lambda k: copy(k, A, second, 4, device(up, p))
+    up_second = lambda k: copy(k, B, B, 5, device(up, p))
+    down_own = lambda k: copy(k, p, C, 6, device(down, p))
+    every = range(len(parts))
+
+    def arrived(slot, k):
+        copy(k, slot, slot, 0, device(z, core_p)).wait_recv()
+
+    for k in every:
+        pl.when(z <= 1)(lambda: up_own(k).start())
+        pl.when(z == 3)(lambda: down_own(k).start())
+        x_own(k).start()
+    for k in every:
+        core_own(k).start()
+
+    def tag_lanes(slot):
+        return held[slot, pl.ds(rows, TAG_ROWS), pl.ds(0, rows)].astype(jnp.float32)[0:1]
+
+    def tag_down(slot):
+        return jnp.broadcast_to(tag_lanes(slot), (128, rows)).T
+
+    def compare(slot, own, first):
+        tags = tag_down(slot)
+        tags = jnp.concatenate([tags] * (rows // 128), axis=1)
+
+        def step(q, best):
+            similar = lax.dot_general(
+                held[slot, pl.ds(0, rows), :],
+                held[q, pl.ds(0, rows), :],
+                (((1,), (1,)), ((), ())),
+                preferred_element_type=jnp.float32,
+            )
+            other = tag_lanes(q)
+            match = tags == jnp.where(other < 0, -2.0, other)
+            if own:
+                here = lax.broadcasted_iota(jnp.int32, (rows, rows), 0)
+                there = lax.broadcasted_iota(jnp.int32, (rows, rows), 1)
+                match = match & (here + jnp.where(q == p, 0, rows) != there)
+            similar = jnp.where(match, similar, -1.0)
+            if not own:
+                top = jnp.broadcast_to(jnp.max(similar, axis=0, keepdims=True), (8, rows))
+                cols[q] = top if first else jnp.maximum(cols[q], top)
+            for i in range(rows // 128):
+                best = jnp.maximum(best, similar[:, i * 128:(i + 1) * 128])
+            return best
+
+        best = lax.fori_loop(0, TEAM, step, jnp.full((rows, 128), -1.0, jnp.float32))
+        return jnp.broadcast_to(jnp.max(best.T, axis=0, keepdims=True), (8, rows))
+
+    def back(n, target, to):
+        return pltpu.make_async_remote_copy(
+            src_ref=outbox.at[n],
+            dst_ref=inbox.at[target],
+            send_sem=back_send.at[n],
+            recv_sem=back_recv.at[target],
+            device_id=to,
+            device_id_type=MESH,
+        )
+
+    back_a = lambda: back(0, z, device(jnp.where(z == 1, 0, 1), p))
+    back_b = lambda: back(1, z, device(0, p))
+    back_c = lambda: back(2, z, device(3, p))
+    back_q = lambda k: back(2 + k, PLANES + p, device(z, (p + k) % TEAM))
+
+    def returned(target):
+        back(0, target, device(z, core_p)).wait_recv()
+
+    for k in every:
+        @pl.when(z >= 1)
+        def _():
+            arrived(A, k)
+            pl.when(z <= 2)(lambda: up_first(k).start())
+
+        arrived(x_p, k)
+        core_pass(k).start()
+    for k in every:
+        arrived(core_p, k)
+    for k in every:
+        arrived(diag_p, k)
+
+    @pl.when(z >= 1)
+    def _():
+        outbox[0] = compare(A, False, True)
+        back_a().start()
+
+    closest = compare(p, True, False)
+
+    @pl.when(z == 2)
+    def _():
+        for k in every:
+            arrived(C, k)
+        outbox[2] = compare(C, False, False)
+        back_c().start()
+
+    @pl.when(z >= 2)
+    def _():
+        for k in every:
+            arrived(B, k)
+            pl.when(z == 2)(lambda: up_second(k).start())
+        outbox[1] = compare(B, False, False)
+        back_b().start()
+
+    @pl.when(z >= 1)
+    def _():
+        for k in range(1, TEAM):
+            outbox[2 + k] = cols[(p + k) % TEAM]
+            back_q(k).start()
+
+    out_ref[...] = closest
+
+    @pl.when(z >= 1)
+    def _():
+        best = cols[p]
+        for k in range(1, TEAM):
+            returned(PLANES + (p + k) % TEAM)
+            best = jnp.maximum(best, inbox[PLANES + (p + k) % TEAM])
+        out_ref[...] = jnp.maximum(out_ref[...], best)
+
+    for source, readers in ((1, z == 0), (2, (z == 0) | (z == 1) | (z == 3)), (3, z <= 1)):
+        @pl.when(readers)
+        def _():
+            returned(source)
+            out_ref[...] = jnp.maximum(out_ref[...], inbox[source])
+
+    for k in every:
+        core_own(k).wait_send()
+        x_own(k).wait_send()
+        core_pass(k).wait_send()
+        pl.when(z <= 1)(lambda: up_own(k).wait_send())
+        pl.when((z == 1) | (z == 2))(lambda: up_first(k).wait_send())
+        pl.when(z == 2)(lambda: up_second(k).wait_send())
+        pl.when(z == 3)(lambda: down_own(k).wait_send())
+
+    @pl.when(z >= 1)
+    def _():
+        back_a().wait_send()
+        for k in range(1, TEAM):
+            back_q(k).wait_send()
+
+    pl.when(z >= 2)(lambda: back_b().wait_send())
+    pl.when(z == 2)(lambda: back_c().wait_send())
+
+
+def in_planes(embeddings, destination, valid_row):
+    rows, width = embeddings.shape
+    tag = jnp.where(valid_row == 1, destination[:, 0] // TEAM, -1).astype(jnp.bfloat16)
+    count = len(pieces(rows, width))
+    vmem = pl.BlockSpec(memory_space=pltpu.VMEM)
+    closest = pl.pallas_call(
+        kernel,
+        out_shape=jax.ShapeDtypeStruct((8, rows), jnp.float32),
+        in_specs=[vmem, vmem],
+        out_specs=vmem,
+        scratch_shapes=[
+            pltpu.VMEM((TEAM + 3, rows + TAG_ROWS, width), jnp.bfloat16),
+            pltpu.VMEM((TEAM, 8, rows), jnp.float32),
+            pltpu.VMEM((6, 8, rows), jnp.float32),
+            pltpu.VMEM((PLANES + TEAM, 8, rows), jnp.float32),
+            pltpu.SemaphoreType.DMA((7, count)),
+            pltpu.SemaphoreType.DMA((7, count)),
+            pltpu.SemaphoreType.DMA((6,)),
+            pltpu.SemaphoreType.DMA((PLANES + TEAM,)),
+        ],
+        compiler_params=pltpu.CompilerParams(
+            collective_id=0, has_side_effects=True, vmem_limit_bytes=32 * 1024 * 1024
+        ),
+    )(embeddings, jnp.broadcast_to(tag[None, :], (TAG_ROWS, rows)))
+    return closest[0]
+
+
 def solution(mesh):
     return jax.shard_map(
-        on_device,
+        in_planes if mesh.shape["cg"] == PLANES * TEAM else on_device,
         mesh=mesh,
         in_specs=(P(("groups", "cg"), None), P(("groups", "cg"), None), P(("groups", "cg"))),
         out_specs=P(("groups", "cg")),

time: 110 us -> 46.1 us (0.42)
  waiting for transfers between devices: 47.7 us -> 0 us
  Pallas kernels: 0 us -> 42.9 us
  blocking collectives: 32 us -> 0 us
  starting transfers between devices: 13.6 us -> 0 us
  matrix products: 4.94 us -> 0 us
  local copies, waits for them, and re-layouts: 6.91 us -> 2.29 us
  other arithmetic: 3.96 us -> 0.69 us
    pallas_call x0 -> x1, Pallas kernels: none -> 42.9 us  [in_planes(): pl.pallas_call(kernel, out_shape=jax.ShapeDtypeStruct((8, rows), jnp.floa...]
    ppermute x3 -> x0, waiting for transfers between devices: 36.9 us -> none  [from_partner(): lax.ppermute(array, axis, [(i, i ^ 1 << stride) for i in range(lax.axis_s...]
    all_to_all x1 -> x0, blocking collectives: 32 us -> none  [on_device(): lax.all_to_all(outgoing.reshape(groups, capacity, feat_width), 'cg', spli...]
    all_to_all x2 -> x0, waiting for transfers between devices: 10.8 us -> none  [the longest x1 6.39 us: on_device(): lax.all_to_all(closest.reshape(groups, capacity), 'cg', split_axis=0, con...]
    all_to_all x2 -> x0, starting transfers between devices: 10.4 us -> none  [the longest x1 5.54 us: on_device(): lax.all_to_all(closest.reshape(groups, capacity), 'cg', split_axis=0, con...]
    dot_general x5 -> x0, matrix products: 4.94 us -> none  [the longest x4 4.74 us: closest_in(): jnp.einsum('id,jd->ij', own_rows, other_rows, preferred_element_type=jnp....]
    ppermute x3 -> x0, starting transfers between devices: 3.19 us -> none  [from_partner(): lax.ppermute(array, axis, [(i, i ^ 1 << stride) for i in range(lax.axis_s...]
    gather x1 -> x0, local copies, waits for them, and re-layouts: 2.5 us -> none  [on_device(): return answers.reshape(slot_count)[row_slot]]
  transfers between devices with their start and end apart: 5 -> 0, of which waited for: 4 -> 0; matrix products, arithmetic and copies ran while one was open for 6% -> 0% of each run, Pallas kernels for 0% -> 0%
where the time goes in v1:
time: 46.1 us; the launch traced here: 45.9 us
  Pallas kernels  42.9 us (93%)
  local copies, waits for them, and re-layouts  2.29 us (5%)
  other arithmetic  0.69 us (1%)
    pallas_call x1, Pallas kernels, in_planes(): pl.pallas_call(kernel, out_shape=jax.ShapeDtypeStruct((8, rows), jnp.floa...  42.9 us
    unnamed x4, local copies, waits for them, and re-layouts  1.71 us

profile of v1, /device:TPU:0, one launch (start us, length us, event | category | flops | bytes accessed | tf_op | source)
XLA Modules:
  0.0 45.9 jit_solution(9775415208325986768)
XLA Ops:
  0.0 0.0 copy-start.1
  0.0 0.7 %copy-done.1 = s32[256]{0:T(256)S(1)} copy-done((s32[256]{0:T(256)S(1)}, s32[256]{0:T(256)}, u32[]{:S(2)}) %copy-start.1) | copy-done | bytes 1048
  0.7 0.7 %fusion = bf16[256]{0:T(256)(128)(2,1)S(1)} fusion(s32[256]{0:T(256)S(1)} %copy-done.1, s32[256]{0:T(256)} %bitcast.2), kind=kLoop, calls=%fused_computation.5 | loop fusion | flops 4608 | bytes 2560 | tf_op jit(solution)/shard_map/convert_element_type | solution.py:311
  1.4 0.0 copy-start
  1.4 1.0 %copy-done = bf16[256,1024]{1,0:T(8,128)(2,1)S(1)} copy-done((bf16[256,1024]{1,0:T(8,128)(2,1)S(1)}, bf16[256,1024]{1,0:T(8,128)(2,1)}, u32[]{:S(2)}) %copy-start) | copy-done | bytes 524312
  2.4 42.9 %shard_map.37 = f32[8,256]{1,0:T(8,128)S(1)} custom-call(bf16[256,1024]{1,0:T(8,128)(2,1)S(1)} %copy-done, bf16[16,256]{1,0:T(8,128)(2,1)S(1)} %broadcast_in_dim.4.tag_ref), custom_call_target="tpu_custom_call" | custom-call | tf_op jit(solution)/shard_map/pallas_call | solution.py:314
  45.3 0.6 %slice.3 = f32[1,256]{1,0:T(1,128)} slice(f32[8,256]{1,0:T(8,128)S(1)} %shard_map.37), slice={[0:1], [0:256]} | slice | bytes 2048 | tf_op jit(solution)/shard_map/slice | solution.py:333
  (1 shorter events, 0.0 us)
Async XLA Ops:
  0.0 0.7 %copy-start.1 = (s32[256]{0:T(256)S(1)}, s32[256]{0:T(256)}, u32[]{:S(2)}) copy-start(s32[256]{0:T(256)} %param.5) | copy-start | bytes 3076
  1.4 1.0 %copy-start = (bf16[256,1024]{1,0:T(8,128)(2,1)S(1)}, bf16[256,1024]{1,0:T(8,128)(2,1)}, u32[]{:S(2)}) copy-start(bf16[256,1024]{1,0:T(8,128)(2,1)} %emb_ref.1) | copy-start | bytes 1572868

commit v2 on v1

--- a/solution.py
+++ b/solution.py
@@ -181,16 +181,13 @@
     def tag_lanes(slot):
         return held[slot, pl.ds(rows, TAG_ROWS), pl.ds(0, rows)].astype(jnp.float32)[0:1]
 
-    def tag_down(slot):
-        return jnp.broadcast_to(tag_lanes(slot), (128, rows)).T
-
-    def compare(slot, own, first):
-        tags = tag_down(slot)
+    def compare(slot, own, first, start=0, size=rows):
+        tags = jnp.broadcast_to(tag_lanes(slot)[:, start:start + size], (128, size)).T
         tags = jnp.concatenate([tags] * (rows // 128), axis=1)
 
         def step(q, best):
             similar = lax.dot_general(
-                held[slot, pl.ds(0, rows), :],
+                held[slot, pl.ds(start, size), :],
                 held[q, pl.ds(0, rows), :],
                 (((1,), (1,)), ((), ())),
                 preferred_element_type=jnp.float32,
@@ -198,8 +195,8 @@
             other = tag_lanes(q)
             match = tags == jnp.where(other < 0, -2.0, other)
             if own:
-                here = lax.broadcasted_iota(jnp.int32, (rows, rows), 0)
-                there = lax.broadcasted_iota(jnp.int32, (rows, rows), 1)
+                here = lax.broadcasted_iota(jnp.int32, (size, rows), 0)
+                there = lax.broadcasted_iota(jnp.int32, (size, rows), 1)
                 match = match & (here + jnp.where(q == p, 0, rows) != there)
             similar = jnp.where(match, similar, -1.0)
             if not own:
@@ -209,8 +206,8 @@
                 best = jnp.maximum(best, similar[:, i * 128:(i + 1) * 128])
             return best
 
-        best = lax.fori_loop(0, TEAM, step, jnp.full((rows, 128), -1.0, jnp.float32))
-        return jnp.broadcast_to(jnp.max(best.T, axis=0, keepdims=True), (8, rows))
+        best = lax.fori_loop(0, TEAM, step, jnp.full((size, 128), -1.0, jnp.float32))
+        return jnp.broadcast_to(jnp.max(best.T, axis=0, keepdims=True), (8, size))
 
     def back(n, target, to):
         return pltpu.make_async_remote_copy(
@@ -248,7 +245,16 @@
         outbox[0] = compare(A, False, True)
         back_a().start()
 
-    closest = compare(p, True, False)
+    def pump(k):
+        @pl.when(z >= 2)
+        def _():
+            arrived(B, k)
+            pl.when(z == 2)(lambda: up_second(k).start())
+
+    pump(0)
+    pump(1)
+    out_ref[...] = compare(p, True, False)
+    pump(2)
 
     @pl.when(z == 2)
     def _():
@@ -257,12 +263,18 @@
         outbox[2] = compare(C, False, False)
         back_c().start()
 
+    half = rows // 2
+
     @pl.when(z >= 2)
     def _():
-        for k in every:
-            arrived(B, k)
-            pl.when(z == 2)(lambda: up_second(k).start())
-        outbox[1] = compare(B, False, False)
+        outbox[1, :, pl.ds(0, half)] = compare(B, False, False, 0, half)
+
+    pump(3)
+    pump(4)
+
+    @pl.when(z >= 2)
+    def _():
+        outbox[1, :, pl.ds(half, half)] = compare(B, False, False, half, half)
         back_b().start()
 
     @pl.when(z >= 1)
@@ -270,8 +282,6 @@
         for k in range(1, TEAM):
             outbox[2 + k] = cols[(p + k) % TEAM]
             back_q(k).start()
-
-    out_ref[...] = closest
 
     @pl.when(z >= 1)
     def _():

time: 46.1 us -> 43.9 us (0.952)
  Pallas kernels: 42.9 us -> 40.7 us
    pallas_call x1, Pallas kernels: 42.9 us -> 40.7 us  [in_planes(): pl.pallas_call(kernel, out_shape=jax.ShapeDtypeStruct((8, rows), jnp.floa...]
where the time goes in v2:
time: 43.9 us; the launch traced here: 43.7 us
  Pallas kernels  40.7 us (93%)
  local copies, waits for them, and re-layouts  2.29 us (5%)
  other arithmetic  0.69 us (2%)
    pallas_call x1, Pallas kernels, in_planes(): pl.pallas_call(kernel, out_shape=jax.ShapeDtypeStruct((8, rows), jnp.floa...  40.7 us
    unnamed x4, local copies, waits for them, and re-layouts  1.71 us

profile of v2, /device:TPU:0, one launch (start us, length us, event | category | flops | bytes accessed | tf_op | source)
XLA Modules:
  0.0 43.7 jit_solution(14028391002495721515)
XLA Ops:
  0.0 0.0 copy-start.1
  0.0 0.7 %copy-done.1 = s32[256]{0:T(256)S(1)} copy-done((s32[256]{0:T(256)S(1)}, s32[256]{0:T(256)}, u32[]{:S(2)}) %copy-start.1) | copy-done | bytes 1048
  0.7 0.7 %fusion = bf16[256]{0:T(256)(128)(2,1)S(1)} fusion(s32[256]{0:T(256)S(1)} %copy-done.1, s32[256]{0:T(256)} %bitcast.2), kind=kLoop, calls=%fused_computation.5 | loop fusion | flops 4608 | bytes 2560 | tf_op jit(solution)/shard_map/convert_element_type | solution.py:321
  1.4 0.0 copy-start
  1.4 1.0 %copy-done = bf16[256,1024]{1,0:T(8,128)(2,1)S(1)} copy-done((bf16[256,1024]{1,0:T(8,128)(2,1)S(1)}, bf16[256,1024]{1,0:T(8,128)(2,1)}, u32[]{:S(2)}) %copy-start) | copy-done | bytes 524312
  2.4 40.7 %shard_map.37 = f32[8,256]{1,0:T(8,128)S(1)} custom-call(bf16[256,1024]{1,0:T(8,128)(2,1)S(1)} %copy-done, bf16[16,256]{1,0:T(8,128)(2,1)S(1)} %broadcast_in_dim.4.tag_ref), custom_call_target="tpu_custom_call" | custom-call | tf_op jit(solution)/shard_map/pallas_call | solution.py:324
  43.1 0.6 %slice.3 = f32[1,256]{1,0:T(1,128)} slice(f32[8,256]{1,0:T(8,128)S(1)} %shard_map.37), slice={[0:1], [0:256]} | slice | bytes 2048 | tf_op jit(solution)/shard_map/slice | solution.py:343
  (1 shorter events, 0.0 us)
Async XLA Ops:
  0.0 0.7 %copy-start.1 = (s32[256]{0:T(256)S(1)}, s32[256]{0:T(256)}, u32[]{:S(2)}) copy-start(s32[256]{0:T(256)} %param.5) | copy-start | bytes 3076
  1.4 1.0 %copy-start = (bf16[256,1024]{1,0:T(8,128)(2,1)S(1)}, bf16[256,1024]{1,0:T(8,128)(2,1)}, u32[]{:S(2)}) copy-start(bf16[256,1024]{1,0:T(8,128)(2,1)} %emb_ref.1) | copy-start | bytes 1572868

commit v3 on v2

--- a/solution.py
+++ b/solution.py
@@ -106,9 +106,9 @@
 
 MESH = pl.DeviceIdType.MESH
 PLANES = 4
-CHUNKS = 4
+CHUNKS = 8
 TAG_ROWS = 16
-A, B, C = 4, 5, 6
+A, B, C, D = 4, 5, 6, 7
 
 
 def pieces(row_count, feat_width):
@@ -121,19 +121,31 @@
     parts = pieces(rows, width)
     group = lax.axis_index("groups")
     me = lax.axis_index("cg")
-    z, p = me // TEAM, me % TEAM
+    other = 1 - group
+
+    def turned(plane, of):
+        return plane + of * (PLANES - 1 - 2 * plane)
+
+    z, p = turned(me // TEAM, group), me % TEAM
     core_p = p + 1 - 2 * (p % 2)
     x_p = (p + 2) % TEAM
     diag_p = (core_p + 2) % TEAM
 
     def device(plane, place):
-        return (group, plane * TEAM + place)
+        return (group, turned(plane, group) * TEAM + place)
+
+    def across(plane):
+        return (other, turned(plane, other) * TEAM + p)
 
     barrier = pltpu.get_barrier_semaphore()
     for k in range(1, TEAM):
         pl.semaphore_signal(barrier, inc=1, device_id=device(z, (p + k) % TEAM), device_id_type=MESH)
     for k in range(1, PLANES):
         pl.semaphore_signal(barrier, inc=1, device_id=device((z + k) % PLANES, p), device_id_type=MESH)
+    for k in range(1, PLANES):
+        @pl.when((z == 2) | ((z > 0) & (k == 2)))
+        def _():
+            pl.semaphore_signal(barrier, inc=1, device_id=across(k), device_id_type=MESH)
 
     for i in range(4):
         block = pl.ds(i * (rows // 4), rows // 4)
@@ -141,7 +153,8 @@
         inv_scale = lax.rsqrt(jnp.mean(values * values, axis=1, keepdims=True) + epsilon)
         held[p, block, :] = (values * inv_scale * width ** (-0.5)).astype(jnp.bfloat16)
     held[p, pl.ds(rows, TAG_ROWS), pl.ds(0, rows)] = tag_ref[...]
-    pl.semaphore_wait(barrier, TEAM - 1 + PLANES - 1)
+    greeted = jnp.where(z == 2, PLANES - 1, jnp.where(z == 0, 0, 1))
+    pl.semaphore_wait(barrier, TEAM - 1 + PLANES - 1 + greeted)
 
     def piece(slot, k):
         start, size, lanes = parts[k]
@@ -166,13 +179,19 @@
     up_first = lambda k: copy(k, A, second, 4, device(up, p))
     up_second = lambda k: copy(k, B, B, 5, device(up, p))
     down_own = lambda k: copy(k, p, C, 6, device(down, p))
+    out_relay = lambda k: copy(k, p, D, 7, across(2))
+    relay_2 = lambda k: copy(k, D, A, 8, across(2))
+    relay_3 = lambda k: copy(k, D, A, 9, across(3))
     every = range(len(parts))
+    relayed = every[len(parts) - CHUNKS // 2:]
 
     def arrived(slot, k):
         copy(k, slot, slot, 0, device(z, core_p)).wait_recv()
 
     for k in every:
-        pl.when(z <= 1)(lambda: up_own(k).start())
+        pl.when((z == 0) if k in relayed else (z <= 1))(lambda: up_own(k).start())
+        if k in relayed:
+            pl.when(z == 1)(lambda: out_relay(k).start())
         pl.when(z == 3)(lambda: down_own(k).start())
         x_own(k).start()
     for k in every:
@@ -211,8 +230,8 @@
 
     def back(n, target, to):
         return pltpu.make_async_remote_copy(
-            src_ref=outbox.at[n],
-            dst_ref=inbox.at[target],
+            src_ref=outbox.at[n, pl.ds(0, 1)],
+            dst_ref=inbox.at[target, pl.ds(0, 1)],
             send_sem=back_send.at[n],
             recv_sem=back_recv.at[target],
             device_id=to,
@@ -227,34 +246,43 @@
     def returned(target):
         back(0, target, device(z, core_p)).wait_recv()
 
-    for k in every:
-        @pl.when(z >= 1)
-        def _():
-            arrived(A, k)
-            pl.when(z <= 2)(lambda: up_first(k).start())
-
-        arrived(x_p, k)
-        core_pass(k).start()
-    for k in every:
-        arrived(core_p, k)
-    for k in every:
-        arrived(diag_p, k)
-
-    @pl.when(z >= 1)
-    def _():
-        outbox[0] = compare(A, False, True)
-        back_a().start()
-
     def pump(k):
         @pl.when(z >= 2)
         def _():
             arrived(B, k)
             pl.when(z == 2)(lambda: up_second(k).start())
 
-    pump(0)
-    pump(1)
+    for k in every:
+        if k + len(relayed) in relayed:
+            @pl.when(z == 2)
+            def _():
+                arrived(D, k + len(relayed))
+                relay_2(k + len(relayed)).start()
+                relay_3(k + len(relayed)).start()
+
+        if k in relayed:
+            pump(k - relayed[0])
+
+        @pl.when(z >= 1)
+        def _():
+            arrived(A, k)
+            pl.when((z == 1) if k in relayed else (z <= 2))(lambda: up_first(k).start())
+
+    for k in every:
+        arrived(x_p, k)
+        core_pass(k).start()
+    for k in every:
+        arrived(core_p, k)
+    for k in every:
+        arrived(diag_p, k)
+
+    @pl.when(z >= 1)
+    def _():
+        outbox[0] = compare(A, False, True)
+        back_a().start()
+
     out_ref[...] = compare(p, True, False)
-    pump(2)
+    pump(4)
 
     @pl.when(z == 2)
     def _():
@@ -269,8 +297,8 @@
     def _():
         outbox[1, :, pl.ds(0, half)] = compare(B, False, False, 0, half)
 
-    pump(3)
-    pump(4)
+    for k in every[5:]:
+        pump(k)
 
     @pl.when(z >= 2)
     def _():
@@ -288,21 +316,25 @@
         best = cols[p]
         for k in range(1, TEAM):
             returned(PLANES + (p + k) % TEAM)
-            best = jnp.maximum(best, inbox[PLANES + (p + k) % TEAM])
+            best = jnp.maximum(best, inbox[PLANES + (p + k) % TEAM, pl.ds(0, 1)])
         out_ref[...] = jnp.maximum(out_ref[...], best)
 
     for source, readers in ((1, z == 0), (2, (z == 0) | (z == 1) | (z == 3)), (3, z <= 1)):
         @pl.when(readers)
         def _():
             returned(source)
-            out_ref[...] = jnp.maximum(out_ref[...], inbox[source])
+            out_ref[...] = jnp.maximum(out_ref[...], inbox[source, pl.ds(0, 1)])
 
     for k in every:
         core_own(k).wait_send()
         x_own(k).wait_send()
         core_pass(k).wait_send()
-        pl.when(z <= 1)(lambda: up_own(k).wait_send())
-        pl.when((z == 1) | (z == 2))(lambda: up_first(k).wait_send())
+        pl.when((z == 0) if k in relayed else (z <= 1))(lambda: up_own(k).wait_send())
+        pl.when((z == 1) if k in relayed else ((z == 1) | (z == 2)))(lambda: up_first(k).wait_send())
+        if k in relayed:
+            pl.when(z == 1)(lambda: out_relay(k).wait_send())
+            pl.when(z == 2)(lambda: relay_2(k).wait_send())
+            pl.when(z == 2)(lambda: relay_3(k).wait_send())
         pl.when(z == 2)(lambda: up_second(k).wait_send())
         pl.when(z == 3)(lambda: down_own(k).wait_send())
 
@@ -327,12 +359,12 @@
         in_specs=[vmem, vmem],
         out_specs=vmem,
         scratch_shapes=[
-            pltpu.VMEM((TEAM + 3, rows + TAG_ROWS, width), jnp.bfloat16),
+            pltpu.VMEM((TEAM + 4, rows + TAG_ROWS, width), jnp.bfloat16),
             pltpu.VMEM((TEAM, 8, rows), jnp.float32),
             pltpu.VMEM((6, 8, rows), jnp.float32),
             pltpu.VMEM((PLANES + TEAM, 8, rows), jnp.float32),
-            pltpu.SemaphoreType.DMA((7, count)),
-            pltpu.SemaphoreType.DMA((7, count)),
+            pltpu.SemaphoreType.DMA((10, count)),
+            pltpu.SemaphoreType.DMA((TEAM + 4, count)),
             pltpu.SemaphoreType.DMA((6,)),
             pltpu.SemaphoreType.DMA((PLANES + TEAM,)),
         ],
@@ -345,7 +377,7 @@
 
 def solution(mesh):
     return jax.shard_map(
-        in_planes if mesh.shape["cg"] == PLANES * TEAM else on_device,
+        in_planes if dict(mesh.shape) == {"groups": 2, "cg": PLANES * TEAM} else on_device,
         mesh=mesh,
         in_specs=(P(("groups", "cg"), None), P(("groups", "cg"), None), P(("groups", "cg"))),
         out_specs=P(("groups", "cg")),

time: 43.9 us -> 42.5 us (0.968)
  Pallas kernels: 40.7 us -> 39.4 us
    pallas_call x1, Pallas kernels: 40.7 us -> 39.4 us  [in_planes(): pl.pallas_call(kernel, out_shape=jax.ShapeDtypeStruct((8, rows), jnp.floa...]
where the time goes in v3:
time: 42.5 us; the launch traced here: 42.4 us
  Pallas kernels  39.4 us (93%)
  local copies, waits for them, and re-layouts  2.29 us (5%)
  other arithmetic  0.69 us (2%)
    pallas_call x1, Pallas kernels, in_planes(): pl.pallas_call(kernel, out_shape=jax.ShapeDtypeStruct((8, rows), jnp.floa...  39.4 us
    unnamed x4, local copies, waits for them, and re-layouts  1.71 us

profile of v3, /device:TPU:0, one launch (start us, length us, event | category | flops | bytes accessed | tf_op | source)
XLA Modules:
  0.0 42.4 jit_solution(3703963232326663241)
XLA Ops:
  0.0 0.0 copy-start.1
  0.0 0.7 %copy-done.1 = s32[256]{0:T(256)S(1)} copy-done((s32[256]{0:T(256)S(1)}, s32[256]{0:T(256)}, u32[]{:S(2)}) %copy-start.1) | copy-done | bytes 1048
  0.7 0.7 %fusion = bf16[256]{0:T(256)(128)(2,1)S(1)} fusion(s32[256]{0:T(256)S(1)} %copy-done.1, s32[256]{0:T(256)} %bitcast.2), kind=kLoop, calls=%fused_computation.5 | loop fusion | flops 4608 | bytes 2560 | tf_op jit(solution)/shard_map/convert_element_type | solution.py:353
  1.4 0.0 copy-start
  1.4 1.0 %copy-done = bf16[256,1024]{1,0:T(8,128)(2,1)S(1)} copy-done((bf16[256,1024]{1,0:T(8,128)(2,1)S(1)}, bf16[256,1024]{1,0:T(8,128)(2,1)}, u32[]{:S(2)}) %copy-start) | copy-done | bytes 524312
  2.4 39.4 %shard_map.37 = f32[8,256]{1,0:T(8,128)S(1)} custom-call(bf16[256,1024]{1,0:T(8,128)(2,1)S(1)} %copy-done, bf16[16,256]{1,0:T(8,128)(2,1)S(1)} %broadcast_in_dim.4.tag_ref), custom_call_target="tpu_custom_call" | custom-call | tf_op jit(solution)/shard_map/pallas_call | solution.py:356
  41.8 0.6 %slice.3 = f32[1,256]{1,0:T(1,128)} slice(f32[8,256]{1,0:T(8,128)S(1)} %shard_map.37), slice={[0:1], [0:256]} | slice | bytes 2048 | tf_op jit(solution)/shard_map/slice | solution.py:375
  (1 shorter events, 0.0 us)
Async XLA Ops:
  0.0 0.7 %copy-start.1 = (s32[256]{0:T(256)S(1)}, s32[256]{0:T(256)}, u32[]{:S(2)}) copy-start(s32[256]{0:T(256)} %param.5) | copy-start | bytes 3076
  1.4 1.0 %copy-start = (bf16[256,1024]{1,0:T(8,128)(2,1)S(1)}, bf16[256,1024]{1,0:T(8,128)(2,1)}, u32[]{:S(2)}) copy-start(bf16[256,1024]{1,0:T(8,128)(2,1)} %emb_ref.1) | copy-start | bytes 1572868
